TPU v7x, 512 devices: a whole 4x8x8 slice. The times are simulated.
512 devices in a mesh: row: 16 (over y, core), col: 16 (over z, x_lo), depth: 2 (over x_hi).
Axes of the slice: x: 4 (x_hi: 2, x_lo: 2; x = x_hi * 2 + x_lo), y: 8, z: 8, core: 2. Of those that a mesh axis runs over, the one named last changes fastest.
Arguments:
- tokens: bfloat16 [512, 8192], P(('col', 'depth'), 'row'), may hold values from -6 to 6
- grad_output: bfloat16 [512, 8192], P(('col', 'depth'), 'row'), may hold values from -0.21191406 to 0.21191406
- gate_weight: bfloat16 [8192, 16384], P('row', 'col'), may hold values from -0.0625 to 0.0625
- up_weight: bfloat16 [8192, 16384], P('row', 'col'), may hold values from -0.0625 to 0.0625
- down_weight: bfloat16 [16384, 8192], P('col', 'row'), may hold values from -0.046875 to 0.046875
Outputs:
- input_grad: bfloat16 [512, 8192], P(('col', 'depth'), 'row')
- gate_grad: bfloat16 [8192, 16384], P('row', ('col', 'depth'))
- up_grad: bfloat16 [8192, 16384], P('row', ('col', 'depth'))
- down_grad: bfloat16 [16384, 8192], P(('col', 'depth'), 'row')
All inputs are finite; a program needn't handle non-finite values.
Results may differ from a plain program's by a relative error of at most 0.0049.
Values may be sent and summed in bfloat16 or wider, within the bound.
A program may use at most 64 MiB of HBM per device.

v0:
```python
import jax
import jax.numpy as jnp
from jax import lax
from jax.sharding import PartitionSpec as P


def contract(left, right, left_dim, right_dim):
    return lax.dot_general(
        left, right, (((left_dim,), (right_dim,)), ((), ())), preferred_element_type=jnp.float32
    )


def halve_layers(tiles):
    return (
        lax.all_to_all(tiles[0], "depth", split_axis=1, concat_axis=0, tiled=True),
        lax.all_to_all(tiles[1], "depth", split_axis=1, concat_axis=0, tiled=True),
        lax.all_to_all(tiles[2], "depth", split_axis=1, concat_axis=0, tiled=True),
    )


def swap_blocks(array, first, second, block):
    width = array.shape[1]
    return array.reshape(first, second, block, width).transpose(1, 0, 2, 3).reshape(-1, width)


def shards(tokens, grad_output, gate_weight, up_weight, down_weight):
    col_count = lax.axis_size("col")
    depth_count = lax.axis_size("depth")
    depth_index = lax.axis_index("depth")
    block = tokens.shape[0]
    width = tokens.shape[1]
    columns = gate_weight.shape[1]
    all_tokens, all_grads = (
        lax.all_gather(tokens, ("col", "depth"), axis=0, tiled=True),
        lax.all_gather(grad_output, ("col", "depth"), axis=0, tiled=True),
    )

    def own_layer(array):
        shaped = array.reshape(col_count, depth_count, block, width)
        return lax.dynamic_index_in_dim(shaped, depth_index, 1, keepdims=False).reshape(
            col_count * block, width
        )

    layer_tokens = own_layer(all_tokens)
    layer_grads = own_layer(all_grads)
    totals = lax.psum(
        jnp.concatenate(
            [
                jnp.dot(layer_tokens, gate_weight, preferred_element_type=jnp.float32),
                jnp.dot(layer_tokens, up_weight, preferred_element_type=jnp.float32),
                contract(layer_grads, down_weight, 1, 1),
            ],
            axis=1,
        ),
        "row",
    )
    gate_pre = totals[:, :columns]
    up_pre = totals[:, columns : 2 * columns]
    hidden_delta = totals[:, 2 * columns :]
    sigma = jax.nn.sigmoid(gate_pre)
    silu_gate = gate_pre * sigma
    hidden = (silu_gate * up_pre).astype(jnp.bfloat16)
    up_delta = (hidden_delta * silu_gate).astype(jnp.bfloat16)
    slope = sigma * (1.0 + gate_pre * (1.0 - sigma))
    gate_delta = (hidden_delta * up_pre * slope).astype(jnp.bfloat16)
    gate_part = gate_delta
    up_part = up_delta
    input_grad = lax.psum_scatter(
        contract(gate_part, gate_weight, 1, 1) + contract(up_part, up_weight, 1, 1),
        "col",
        scatter_dimension=0,
        tiled=True,
    )
    hidden, gate_delta, up_delta = halve_layers((hidden, gate_delta, up_delta))
    order_tokens = swap_blocks(all_tokens, col_count, depth_count, block)
    order_grads = swap_blocks(all_grads, col_count, depth_count, block)
    gate_grad = contract(order_tokens, gate_delta, 0, 0).astype(jnp.bfloat16)
    up_grad = contract(order_tokens, up_delta, 0, 0).astype(jnp.bfloat16)
    down_grad = contract(hidden, order_grads, 0, 0).astype(jnp.bfloat16)
    return (input_grad.astype(jnp.bfloat16), gate_grad, up_grad, down_grad)


def solution(mesh):
    placed = (
        P(("col", "depth"), "row"),
        P(("col", "depth"), "row"),
        P("row", "col"),
        P("row", "col"),
        P("col", "row"),
    )
    return jax.shard_map(
        shards,
        mesh=mesh,
        in_specs=placed,
        out_specs=(
            P(("col", "depth"), "row"),
            P("row", ("col", "depth")),
            P("row", ("col", "depth")),
            P(("col", "depth"), "row"),
        ),
        check_vma=False,
    )
```

profile of v0, /device:TPU:40, one launch (start us, length us, event | category | flops | bytes accessed | tf_op | source)
XLA Modules:
  0.0 383.0 jit_solution(6851076603241402845)
XLA Ops:
  7.2 0.0 all-reduce.2.cloned.1.call-start
  7.2 82.7 %all_gather.6 = bf16[512,512]{1,0:T(8,128)(2,1)S(1)} all-gather(bf16[16,512]{1,0:T(8,128)(2,1)} %param.5), channel_id=1, replica_groups=mesh['row'=16,'col'=16,'depth'=2] {'col','depth'}, dimensions={0}, use_global_device_ids=true | all-gather | bytes 540672 | tf_op jit(solution)/shard_map/all_gather | solution.py:34
  89.9 71.6 %all_gather.7 = bf16[512,512]{1,0:T(8,128)(2,1)S(1)} all-gather(bf16[16,512]{1,0:T(8,128)(2,1)} %param.6), channel_id=1, replica_groups=mesh['row'=16,'col'=16,'depth'=2] {'col','depth'}, dimensions={0}, use_global_device_ids=true | all-gather | bytes 540672 | tf_op jit(solution)/shard_map/all_gather | solution.py:35
  161.6 1.8 fusion.4
  163.4 0.5 fusion.3
  163.9 0.5 fusion.5
  164.4 2.0 pad_maximum_fusion
  166.4 0.0 all-reduce.2.cloned.1.call-update
  166.4 118.6 %all-reduce.2.cloned.1.call-done = f32[256,3072]{1,0:T(8,128)} async-done(((f32[256,3072]{1,0:T(8,128)}), f32[256,3072]{1,0:T(8,128)}) %all-reduce.2.cloned.1.call-update) | async-done | bytes 3145744 | tf_op jit(solution)/shard_map/psum | solution.py:46
  285.0 3.4 multiply_convert_fusion
  288.4 0.8 copy.30
  289.3 4.2 %all-to-all-start.1 = ((bf16[256,2,512]{2,0,1:T(8,128)(2,1)}), bf16[256,2,512]{2,0,1:T(8,128)(2,1)}, u32[]{:S(2)}, u32[]{:S(2)}) async-start(bf16[256,2,512]{2,0,1:T(8,128)(2,1)} %bitcast.60), calls=%async_computation.2 | async-start | bytes 1048576 | tf_op jit(solution)/shard_map/all_to_all | solution.py:17
  293.5 0.0 reduce-scatter.2.cloned.1.call-start
  293.5 0.5 fusion.6
  294.0 1.3 convolution_add_fusion
  295.3 0.0 reduce-scatter.2.cloned.1.call-update
  295.3 1.1 copy.20
  296.4 1.1 copy.17
  297.5 1.9 copy.29
  299.4 0.8 copy.31
  300.2 1.5 all-to-all-done.1
  301.7 3.5 all-to-all-start
  305.2 1.5 fusion.1
  306.7 1.0 copy.22
  307.7 5.6 %all-to-all-done = bf16[256,2,512]{2,0,1:T(8,128)(2,1)S(1)} async-done(((bf16[256,2,512]{2,0,1:T(8,128)(2,1)}), bf16[256,2,512]{2,0,1:T(8,128)(2,1)S(1)}, u32[]{:S(2)}, u32[]{:S(2)}) %all-to-all-start) | async-done | bytes 524320 | tf_op jit(solution)/shard_map/all_to_all | solution.py:16
  313.3 3.5 all-to-all-start.2
  316.8 1.3 fusion
  318.0 2.0 copy.21
  320.1 5.6 %all-to-all-done.2 = bf16[256,2,512]{2,0,1:T(8,128)(2,1)S(1)} async-done(((bf16[256,2,512]{2,0,1:T(8,128)(2,1)}), bf16[256,2,512]{2,0,1:T(8,128)(2,1)S(1)}, u32[]{:S(2)}, u32[]{:S(2)}) %all-to-all-start.2) | async-done | bytes 524320 | tf_op jit(solution)/shard_map/all_to_all | solution.py:15
  325.6 1.3 convolution_convert_fusion
  326.9 47.9 %reduce-scatter.2.cloned.1.call-done = f32[16,512]{1,0:T(8,128)} async-done(((f32[256,512]{1,0:T(8,128)}), f32[16,512]{1,0:T(8,128)}) %reduce-scatter.2.cloned.1.call-update) | async-done | bytes 32784 | tf_op jit(solution)/shard_map/reduce_scatter | solution.py:68
  374.8 1.4 convert_element_type.29
  (11 shorter events, 0.1 us)
Async XLA Ops:
  7.2 156.2 %copy-start = (bf16[512,1024]{1,0:T(8,128)(2,1)S(1)}, bf16[512,1024]{1,0:T(8,128)(2,1)}, u32[]{:S(2)}) copy-start(bf16[512,1024]{1,0:T(8,128)(2,1)} %param.7) | copy-start | bytes 3145732
  7.2 277.8 %all-reduce.2.cloned.1.call-start = ((), (), s32[]{:S(2)}) async-start(), calls=%async_computation.4 | async-start | bytes 6291456 | tf_op jit(solution)/shard_map/psum | solution.py:46
  89.9 73.9 %copy-start.2 = (bf16[512,512]{1,0:T(8,128)(2,1)}, bf16[512,512]{1,0:T(8,128)(2,1)S(1)}, u32[]{:S(2)}) copy-start(bf16[512,512]{1,0:T(8,128)(2,1)S(1)} %all_gather.6) | copy-start | bytes 1572868
  89.9 73.9 %copy-start.4 = (bf16[1024,512]{1,0:T(8,128)(2,1)S(1)}, bf16[1024,512]{1,0:T(8,128)(2,1)}, u32[]{:S(2)}) copy-start(bf16[1024,512]{1,0:T(8,128)(2,1)} %param.9) | copy-start | bytes 3145732
  161.5 2.9 copy-start.3
  288.4 5.6 %copy-start.1 = (bf16[512,1024]{1,0:T(8,128)(2,1)S(1)}, bf16[512,1024]{1,0:T(8,128)(2,1)}, u32[]{:S(2)}) copy-start(bf16[512,1024]{1,0:T(8,128)(2,1)} %param.8) | copy-start | bytes 3145732
  289.3 12.4 %all-to-all-start.1 = ((bf16[256,2,512]{2,0,1:T(8,128)(2,1)}), bf16[256,2,512]{2,0,1:T(8,128)(2,1)}, u32[]{:S(2)}, u32[]{:S(2)}) async-start(bf16[256,2,512]{2,0,1:T(8,128)(2,1)} %bitcast.60), calls=%async_computation.2 | async-start | bytes 1048576 | tf_op jit(solution)/shard_map/all_to_all | solution.py:17
  293.5 81.2 %reduce-scatter.2.cloned.1.call-start = ((), (), s32[]{:S(2)}) async-start(), calls=%async_computation.5 | async-start | bytes 557056 | tf_op jit(solution)/shard_map/reduce_scatter | solution.py:68
  301.7 11.6 %all-to-all-start = ((bf16[256,2,512]{2,0,1:T(8,128)(2,1)}), bf16[256,2,512]{2,0,1:T(8,128)(2,1)S(1)}, u32[]{:S(2)}, u32[]{:S(2)}) async-start(bf16[256,2,512]{2,0,1:T(8,128)(2,1)} %bitcast.50), calls=%async_computation.1 | async-start | bytes 1048576 | tf_op jit(solution)/shard_map/all_to_all | solution.py:16
  313.3 12.4 %all-to-all-start.2 = ((bf16[256,2,512]{2,0,1:T(8,128)(2,1)}), bf16[256,2,512]{2,0,1:T(8,128)(2,1)S(1)}, u32[]{:S(2)}, u32[]{:S(2)}) async-start(bf16[256,2,512]{2,0,1:T(8,128)(2,1)} %bitcast.48), calls=%async_computation.3 | async-start | bytes 1048576 | tf_op jit(solution)/shard_map/all_to_all | solution.py:15
Sparse Core Ops, SparseCore 0:
  166.5 118.4 all-reduce.1
  297.1 77.5 reduce-scatter.1
where the time goes:
time: 384 us; the launch traced here: 383 us
  waiting for transfers between devices  179 us (47%)
  blocking collectives  154 us (40%)
  between operations  14.2 us (4%)
  starting transfers between devices  11.3 us (3%)
  local copies, waits for them, and re-layouts  8.84 us (2%)
  matrix products  8.51 us (2%)
  other arithmetic  6.79 us (2%)
    psum x1, waiting for transfers between devices, shards(): lax.psum(jnp.concatenate([jnp.dot(layer_tokens, gate_weight, preferred_el...  119 us
    all_gather x1, blocking collectives, shards(): lax.all_gather(tokens, ('col', 'depth'), axis=0, tiled=True)  82.7 us
    all_gather x1, blocking collectives, shards(): lax.all_gather(grad_output, ('col', 'depth'), axis=0, tiled=True)  71.6 us
    reduce_scatter x1, waiting for transfers between devices, shards(): lax.psum_scatter(contract(gate_part, gate_weight, 1, 1) + contract(up_par...  47.9 us
  transfers between devices with their start and end apart: 5, of which 5 were waited for; matrix products, arithmetic and copies ran while one was open for 4% of the time, Pallas kernels for 0%

commit v1 on v0

v1 whole, which is shorter than its diff:
```python
import functools

import jax
import jax.numpy as jnp
from jax import lax
from jax.experimental import pallas as pl
from jax.experimental.pallas import tpu as pltpu
from jax.sharding import PartitionSpec as P

MESH = pl.DeviceIdType.MESH
OFFSETS = (0, 1, 3, 2)
BACK = (0, 2, 1, 3)
SUM_SCALE = 2.0**48
GRAD_SCALE = 2.0**30


def encode(value, scale):
    scaled = value * scale
    return (scaled * jnp.abs(scaled)).astype(jnp.bfloat16)


def decode(code, scale):
    wide = code.astype(jnp.float32)
    root = jnp.sqrt(jnp.abs(wide)) * (1.0 / scale)
    return jnp.where(wide < 0.0, -root, root)


def dot(left, right, left_dim, right_dim):
    return lax.dot_general(
        left, right, (((left_dim,), (right_dim,)), ((), ())), preferred_element_type=jnp.float32
    )


def kernel(
    ny, nz,
    tok, grd, wg, wu, wd,
    ig_out, gg_out, ug_out, dg_out,
    xg, wgv, wuv, wdv, wgs, wus, wds, pf, sb, rb, hb, own, ib, jb, zf, zs, zr,
    load_sem, az_send, az_recv, ax_send, ax_recv, as_send, as_recv, ws_send, ws_recv,
    b_send, b_recv, c_send, c_recv, cs_send, cs_recv, dx_send, dx_recv, dz_send, dz_recv,
):
    nx = 4
    block, width = tok.shape
    half = wgv.shape[2]
    rows = nz * block
    r, q, d = lax.axis_index("row"), lax.axis_index("col"), lax.axis_index("depth")
    y, k = r // 2, lax.rem(r, 2)
    z, x = q // 2, d * 2 + lax.rem(q, 2)

    def place(py, pz, px, pk):
        return (py * 2 + pk, pz * 2 + lax.rem(px, 2), px // 2)

    def y_peer(step):
        return place(lax.rem(y + step, ny), z, x, k)

    def z_peer(step):
        return place(y, lax.rem(z + step, nz), x, k)

    def x_peer(step):
        return place(y, z, lax.rem(x + step, nx), k)

    sibling = place(y, z, x, 1 - k)

    def remote(src, dst, send, recv, device):
        return pltpu.make_async_remote_copy(
            src_ref=src, dst_ref=dst, send_sem=send, recv_sem=recv, device_id=device, device_id_type=MESH
        )

    loads = [
        pltpu.make_async_copy(tok, xg.at[k, 0, z, 0], load_sem.at[0]),
        pltpu.make_async_copy(grd, xg.at[k, 0, z, 1], load_sem.at[1]),
    ]
    for side in range(2):
        start = pl.multiple_of(d * (2 * half) + side * half, half)
        loads += [
            pltpu.make_async_copy(wg.at[:, pl.ds(start, half)], wgv.at[side], load_sem.at[2 + side]),
            pltpu.make_async_copy(wu.at[:, pl.ds(start, half)], wuv.at[side], load_sem.at[4 + side]),
            pltpu.make_async_copy(wd.at[pl.ds(start, half)], wdv.at[side], load_sem.at[6 + side]),
        ]
    for load in loads:
        load.start()

    barrier = pltpu.get_barrier_semaphore()

    def signal(device):
        pl.semaphore_signal(barrier, inc=1, device_id=device, device_id_type=MESH)

    signal(sibling)
    for step in range(1, nx):
        signal(x_peer(step))
    for step in range(1, nz):
        signal(z_peer(step))
    for step in range(1, ny):
        signal(y_peer(step))
    loads[0].wait()
    loads[1].wait()
    pl.semaphore_wait(barrier, 1 + (nx - 1) + (nz - 1) + (ny - 1))

    def z_copy(step):
        mine = xg.at[k, 0, z]
        return remote(mine, mine, az_send.at[step - 1], az_recv.at[step - 1], z_peer(step))

    def x_copy(chunk, at):
        return remote(
            xg.at[k, 0, at], xg.at[k, BACK[chunk], at],
            ax_send.at[chunk, at], ax_recv.at[BACK[chunk], at], x_peer(OFFSETS[chunk]),
        )

    def twin_copy(chunk):
        ours = xg.at[k, chunk]
        return remote(ours, ours, as_send.at[chunk], as_recv.at[chunk], sibling)

    order = sorted(range(1, nz), key=lambda s: -min(s, nz - s))
    for step in order:
        z_copy(step).start()
    for chunk in range(1, nx):
        x_copy(chunk, z).start()
    for load in loads[2:]:
        load.wait()
    weights = [
        remote(wgv.at[1 - k], wgs, ws_send.at[0], ws_recv.at[0], sibling),
        remote(wuv.at[1 - k], wus, ws_send.at[1], ws_recv.at[1], sibling),
        remote(wdv.at[1 - k], wds, ws_send.at[2], ws_recv.at[2], sibling),
    ]
    for copy in weights:
        copy.start()
    for step in reversed(order):
        z_copy(step).wait_recv()
        at = lax.rem(z + nz - step, nz)
        for chunk in range(1, nx):
            x_copy(chunk, at).start()
    twin_copy(0).start()
    for copy in weights:
        copy.wait_recv()

    def b_copy(chunk, step):
        return remote(
            sb.at[chunk, lax.rem(y + step, ny)], rb.at[chunk, step - 1],
            b_send.at[chunk, step - 1], b_recv.at[chunk, step - 1], y_peer(step),
        )

    y_order = sorted(range(1, ny), key=lambda s: -min(s, ny - s))
    for chunk in range(nx):
        if chunk > 0:
            for at in range(nz):
                x_copy(BACK[chunk], at).wait_recv()
            twin_copy(chunk).start()
        ours = xg[k, chunk]
        left = ours[:, 0].reshape(rows, width)
        left_grad = ours[:, 1].reshape(rows, width)
        sums = [
            dot(left, wgv[k], 1, 0),
            dot(left, wuv[k], 1, 0),
            dot(left_grad, wdv[k], 1, 1),
        ]
        twin_copy(chunk).wait_recv()
        other = xg[1 - k, chunk]
        right = other[:, 0].reshape(rows, width)
        right_grad = other[:, 1].reshape(rows, width)
        sums[0] += dot(right, wgs[...], 1, 0)
        sums[1] += dot(right, wus[...], 1, 0)
        sums[2] += dot(right_grad, wds[...], 1, 1)
        for part in range(3):
            cols = pl.ds(part * half, half)
            pf[chunk, :, :, cols] = sums[part].reshape(ny, block, half)
            sb[chunk, :, :, cols] = encode(sums[part], SUM_SCALE).reshape(ny, block, half)
        for step in y_order:
            b_copy(chunk, step).start()

    def c_copy(chunk, step):
        mine = hb.at[chunk, k, y]
        return remote(mine, mine, c_send.at[chunk, step - 1], c_recv.at[chunk, step - 1], y_peer(step))

    def half_copy(chunk):
        ours = hb.at[chunk, k]
        return remote(ours, ours, cs_send.at[chunk], cs_recv.at[chunk], sibling)

    for chunk in range(nx):
        for step in range(1, ny):
            b_copy(chunk, step).wait_recv()
        total = pf[chunk, y]
        for step in range(1, ny):
            total += decode(rb[chunk, step - 1], SUM_SCALE)
        gate_pre = total[:, :half]
        up_pre = total[:, half : 2 * half]
        hidden_delta = total[:, 2 * half :]
        sigma = jax.nn.sigmoid(gate_pre)
        silu_gate = gate_pre * sigma
        slope = sigma * (1.0 + gate_pre * (1.0 - sigma))
        hb[chunk, k, y, 0] = (silu_gate * up_pre).astype(jnp.bfloat16)
        hb[chunk, k, y, 1] = (hidden_delta * up_pre * slope).astype(jnp.bfloat16)
        hb[chunk, k, y, 2] = (hidden_delta * silu_gate).astype(jnp.bfloat16)
        for step in y_order:
            c_copy(chunk, step).start()

    def dx_copy(chunk):
        return remote(
            ib.at[chunk], jb.at[BACK[chunk]], dx_send.at[chunk], dx_recv.at[BACK[chunk]], x_peer(OFFSETS[chunk])
        )

    def term(chunk, side):
        gate = hb[chunk, side, :, 1].reshape(rows, half)
        up = hb[chunk, side, :, 2].reshape(rows, half)
        return dot(gate, wgv[side], 1, 1) + dot(up, wuv[side], 1, 1)

    for chunk in (1, 2, 3, 0):
        for step in range(1, ny):
            c_copy(chunk, step).wait_recv()
        half_copy(chunk).start()
        total = term(chunk, k)
        half_copy(chunk).wait_recv()
        total = (total + term(chunk, 1 - k)).reshape(nz, block, width)
        if chunk == 0:
            own[...] = total
        else:
            ib[chunk] = encode(total, GRAD_SCALE)
            dx_copy(chunk).start()

    tokens = nx * rows

    def gradient(out, of_tokens, part):
        left = xg[k, :, :, of_tokens].reshape(tokens, width)
        for side in range(2):
            right = hb[:, side, :, part].reshape(tokens, half)
            out[:, pl.ds(side * half, half)] = dot(left, right, 0, 0).astype(jnp.bfloat16)

    gradient(gg_out, 0, 1)
    for chunk in range(1, nx):
        dx_copy(BACK[chunk]).wait_recv()
    total = own[...]
    for chunk in range(1, nx):
        total += decode(jb[chunk], GRAD_SCALE)
    zf[...] = total
    zs[...] = encode(total, GRAD_SCALE)

    def dz_copy(step):
        return remote(
            zs.at[lax.rem(z + step, nz)], zr.at[step - 1], dz_send.at[step - 1], dz_recv.at[step - 1], z_peer(step)
        )

    for step in order:
        dz_copy(step).start()
    gradient(ug_out, 0, 2)
    right = xg[k, :, :, 1].reshape(tokens, width)
    for side in range(2):
        left = hb[:, side, :, 0].reshape(tokens, half)
        dg_out[pl.ds(side * half, half)] = dot(left, right, 0, 0).astype(jnp.bfloat16)
    for step in range(1, nz):
        dz_copy(step).wait_recv()
    total = zf[z]
    for step in range(1, nz):
        total += decode(zr[step - 1], GRAD_SCALE)
    ig_out[...] = total.astype(jnp.bfloat16)

    for copy in weights:
        copy.wait_send()
    for step in range(1, nz):
        z_copy(step).wait_send()
        dz_copy(step).wait_send()
    for chunk in range(1, nx):
        for at in range(nz):
            x_copy(chunk, at).wait_send()
        dx_copy(chunk).wait_send()
    for chunk in range(nx):
        twin_copy(chunk).wait_send()
        half_copy(chunk).wait_send()
        for step in range(1, ny):
            b_copy(chunk, step).wait_send()
            c_copy(chunk, step).wait_send()


def shards(ny, nz, tokens, grad_output, gate_weight, up_weight, down_weight):
    block, width = tokens.shape
    hidden = gate_weight.shape[1] // 2
    half = hidden // 2
    nx = 4
    bf16, f32 = jnp.bfloat16, jnp.float32
    vmem, dma = pltpu.VMEM, pltpu.SemaphoreType.DMA
    return pl.pallas_call(
        functools.partial(kernel, ny, nz),
        out_shape=(
            jax.ShapeDtypeStruct((block, width), bf16),
            jax.ShapeDtypeStruct((width, hidden), bf16),
            jax.ShapeDtypeStruct((width, hidden), bf16),
            jax.ShapeDtypeStruct((hidden, width), bf16),
        ),
        in_specs=[pl.BlockSpec(memory_space=pl.ANY)] * 5,
        out_specs=[pl.BlockSpec(memory_space=vmem)] * 4,
        scratch_shapes=[
            vmem((2, nx, nz, 2, block, width), bf16),
            vmem((2, width, half), bf16),
            vmem((2, width, half), bf16),
            vmem((2, half, width), bf16),
            vmem((width, half), bf16),
            vmem((width, half), bf16),
            vmem((half, width), bf16),
            vmem((nx, ny, block, 3 * half), f32),
            vmem((nx, ny, block, 3 * half), bf16),
            vmem((nx, ny - 1, block, 3 * half), bf16),
            vmem((nx, 2, ny, 3, block, half), bf16),
            vmem((nz, block, width), f32),
            vmem((nx, nz, block, width), bf16),
            vmem((nx, nz, block, width), bf16),
            vmem((nz, block, width), f32),
            vmem((nz, block, width), bf16),
            vmem((nz - 1, block, width), bf16),
            dma((8,)),
            dma((nz - 1,)), dma((nz - 1,)),
            dma((nx, nz)), dma((nx, nz)),
            dma((nx,)), dma((nx,)),
            dma((3,)), dma((3,)),
            dma((nx, ny - 1)), dma((nx, ny - 1)),
            dma((nx, ny - 1)), dma((nx, ny - 1)),
            dma((nx,)), dma((nx,)),
            dma((nx,)), dma((nx,)),
            dma((nz - 1,)), dma((nz - 1,)),
        ],
        compiler_params=pltpu.CompilerParams(
            collective_id=0, has_side_effects=True, vmem_limit_bytes=60 * 2**20
        ),
        name="ffn_backward",
    )(tokens, grad_output, gate_weight, up_weight, down_weight)


def solution(mesh):
    placed = (
        P(("col", "depth"), "row"),
        P(("col", "depth"), "row"),
        P("row", "col"),
        P("row", "col"),
        P("col", "row"),
    )
    ny, nz = mesh.shape["row"] // 2, mesh.shape["col"] // 2
    return jax.shard_map(
        functools.partial(shards, ny, nz),
        mesh=mesh,
        in_specs=placed,
        out_specs=(
            P(("col", "depth"), "row"),
            P("row", ("col", "depth")),
            P("row", ("col", "depth")),
            P(("col", "depth"), "row"),
        ),
        check_vma=False,
    )
```

time: 384 us -> 87.6 us (0.23)
  the two profiles are of different devices: /device:TPU:40 before, /device:TPU:1 now
where the time goes in v1:
time: 87.6 us; the launch traced here: 87.3 us
  Pallas kernels  81.4 us (93%)
  local copies, waits for them, and re-layouts  5.28 us (6%)
    pallas_call x1, Pallas kernels, shards(): pl.pallas_call(functools.partial(kernel, ny, nz), out_shape=(jax.ShapeDty...  81.4 us
    unnamed x8, local copies, waits for them, and re-layouts  5.28 us

profile of v1, /device:TPU:1, one launch (start us, length us, event | category | flops | bytes accessed | tf_op | source)
XLA Modules:
  0.0 87.3 jit_solution(13201936371609861599)
XLA Ops:
  0.6 81.4 %ffn_backward.1 = (bf16[16,512]{1,0:T(8,128)(2,1)}, bf16[512,512]{1,0:T(8,128)(2,1)}, bf16[512,512]{1,0:T(8,128)(2,1)}, bf16[512,512]{1,0:T(8,128)(2,1)}) custom-call(bf16[16,512]{1,0:T(8,128)(2,1)} %tok.1, bf16[16,512]{1,0:T(8,128)(2,1)} %grd.1, bf16[512,1024]{1,0:T(8,128)(2,1)} %wg.1, bf16[512,1024]{1,0:T(8,128)(2,1)} %wu.1, bf16[1024,512]{1,0:T(8,128)(2,1)} %wd.1), custom_call_target="tpu_custom_call" | custom-call | tf_op jit(solution)/shard_map/ffn_backward/pallas_call | solution.py:279
  82.0 1.3 %copy.13 = bf16[16,512]{1,0:T(8,128)(2,1)} copy(bf16[16,512]{1,0:T(8,128)(2,1)} %get-tuple-element.8) | data formatting | bytes 32768
  83.4 0.0 copy-start.1
  83.4 1.9 %copy.14 = bf16[512,512]{1,0:T(8,128)(2,1)} copy(bf16[512,512]{1,0:T(8,128)(2,1)} %get-tuple-element.9) | data formatting | bytes 1048576
  85.3 0.0 copy-done.1
  85.3 0.0 copy-start
  85.3 0.8 copy.15
  86.1 0.4 copy-done
  86.5 0.8 copy.16
Async XLA Ops:
  83.4 1.9 %copy-start.1 = (bf16[512,512]{1,0:T(8,128)(2,1)S(1)}, bf16[512,512]{1,0:T(8,128)(2,1)}, u32[]{:S(2)}) copy-start(bf16[512,512]{1,0:T(8,128)(2,1)} %get-tuple-element.10) | copy-start | bytes 1572868
  85.3 1.2 %copy-start = (bf16[512,512]{1,0:T(8,128)(2,1)S(1)}, bf16[512,512]{1,0:T(8,128)(2,1)}, u32[]{:S(2)}) copy-start(bf16[512,512]{1,0:T(8,128)(2,1)} %get-tuple-element.11) | copy-start | bytes 1572868

commit v2 on v1

v2 whole, which is shorter than its diff:
```python
import functools

import jax
import jax.numpy as jnp
from jax import lax
from jax.experimental import pallas as pl
from jax.experimental.pallas import tpu as pltpu
from jax.sharding import PartitionSpec as P

MESH = pl.DeviceIdType.MESH
OFFSETS = (0, 1, 3, 2)
BACK = (0, 2, 1, 3)
SUM_SCALE = 2.0**48
GRAD_SCALE = 2.0**30


def encode(value, scale):
    scaled = value * scale
    return (scaled * jnp.abs(scaled)).astype(jnp.bfloat16)


def decode(code, scale):
    wide = code.astype(jnp.float32)
    root = jnp.sqrt(jnp.abs(wide)) * (1.0 / scale)
    return jnp.where(wide < 0.0, -root, root)


def dot(left, right, left_dim, right_dim):
    return lax.dot_general(
        left, right, (((left_dim,), (right_dim,)), ((), ())), preferred_element_type=jnp.float32
    )


STEPS = (
    ("sum", 0), ("fetch", 3), ("fetch", 1), ("sum", 3), ("fetch", 2), ("sum", 1), ("sum", 2),
    ("join", 0), ("join", 3), ("join", 1), ("join", 2), ("gate", 3), ("gate", 1), ("gate", 2), ("gate", 0),
    ("pass", 3), ("pass", 1), ("pass", 2), ("pass", 0),
    ("half", 3), ("half", 1), ("grad", 3), ("half", 2), ("grad", 1), ("half", 0), ("grad", 2), ("grad", 0),
)


def kernel(
    ny, nz,
    tok, grd, wg, wu, wd,
    ig_out, gg_out, ug_out, dg_out,
    xg, wgv, wuv, wdv, wgs, wus, wds, pf, sb, pa, pb, pc, sc, rc, hb, own, ib, jb, zf, zs, zr, ggv, ugv, dgv, igv,
    load_sem, az_send, az_recv, ax_send, ax_recv, as_send, as_recv, ws_send, ws_recv,
    b_send, b_recv, c_send, c_recv, cs_send, cs_recv, dx_send, dx_recv, dz_send, dz_recv,
):
    nx = 4
    block, width = tok.shape
    half = wgv.shape[2]
    rows = nz * block
    r, q, d = lax.axis_index("row"), lax.axis_index("col"), lax.axis_index("depth")
    y, k = r // 2, lax.rem(r, 2)
    z, x = q // 2, d * 2 + lax.rem(q, 2)

    def place(py, pz, px, pk):
        return (py * 2 + pk, pz * 2 + lax.rem(px, 2), px // 2)

    def along_y(step):
        return lax.rem(y + step + ny, ny)

    def along_z(step):
        return lax.rem(z + step + nz, nz)

    def y_peer(step):
        return place(along_y(step), z, x, k)

    def z_peer(step):
        return place(y, along_z(step), x, k)

    def x_peer(step):
        return place(y, z, lax.rem(x + step, nx), k)

    sibling = place(y, z, x, 1 - k)
    far = 2 - 4 * k
    sent = []

    def remote(src, dst, send, recv, device):
        return pltpu.make_async_remote_copy(
            src_ref=src, dst_ref=dst, send_sem=send, recv_sem=recv, device_id=device, device_id_type=MESH
        )

    def start(copy):
        copy.start()
        sent.append(copy)

    loads = [
        pltpu.make_async_copy(tok, xg.at[k, 0, z, 0], load_sem.at[0]),
        pltpu.make_async_copy(grd, xg.at[k, 0, z, 1], load_sem.at[1]),
    ]
    for side in range(2):
        first = pl.multiple_of(d * (2 * half) + side * half, half)
        loads += [
            pltpu.make_async_copy(wg.at[:, pl.ds(first, half)], wgv.at[side], load_sem.at[2 + side]),
            pltpu.make_async_copy(wu.at[:, pl.ds(first, half)], wuv.at[side], load_sem.at[4 + side]),
            pltpu.make_async_copy(wd.at[pl.ds(first, half)], wdv.at[side], load_sem.at[6 + side]),
        ]
    for load in loads:
        load.start()

    barrier = pltpu.get_barrier_semaphore()
    friends = [sibling]
    friends += [z_peer(step) for step in range(1, nz)]
    friends += [x_peer(step) for step in range(1, nx)]
    friends += [y_peer(step) for step in (1, -1, 2, -2)]
    for device in friends:
        pl.semaphore_signal(barrier, inc=1, device_id=device, device_id_type=MESH)
    loads[0].wait()
    loads[1].wait()
    pl.semaphore_wait(barrier, len(friends))

    def ring_copy(buffer, at, peer, send, recv, origin, number, target):
        piece = buffer.at[at(origin)]
        return remote(piece, piece, send.at[number], recv.at[number], peer(target))

    def ring_first(ring):
        for target in (2, -2, 1, -1):
            start(ring_copy(*ring, 0, target % 8, target))

    def ring_second(ring):
        ring_wait(ring, 2)
        ring_wait(ring, 6)
        start(ring_copy(*ring, -far, 4, far))
        start(ring_copy(*ring, -2, 3, 1))
        start(ring_copy(*ring, 2, 5, -1))

    def ring_wait(ring, number):
        ring_copy(*ring, -number, number, 0).wait_recv()

    z_ring = (xg.at[k, 0], along_z, z_peer, az_send.at[0], az_recv.at[0])
    far_ring = (xg.at[k, 3], along_z, z_peer, az_send.at[1], az_recv.at[1])

    def x_copy(chunk, at):
        return remote(
            xg.at[k, 0, at], xg.at[k, BACK[chunk], at],
            ax_send.at[chunk, at], ax_recv.at[BACK[chunk], at], x_peer(OFFSETS[chunk]),
        )

    def twin_copy(chunk):
        ours = xg.at[k, chunk]
        return remote(ours, ours, as_send.at[chunk], as_recv.at[chunk], sibling)

    def spread(number):
        for chunk in (1, 2):
            start(x_copy(chunk, along_z(-number)))

    start(x_copy(3, z))
    ring_first(z_ring)
    spread(0)
    for load in loads[2:]:
        load.wait()
    weights = [
        remote(wgv.at[1 - k], wgs, ws_send.at[0], ws_recv.at[0], sibling),
        remote(wuv.at[1 - k], wus, ws_send.at[1], ws_recv.at[1], sibling),
        remote(wdv.at[1 - k], wds, ws_send.at[2], ws_recv.at[2], sibling),
    ]
    for copy in weights:
        start(copy)
    for number in (1, 7):
        ring_wait(z_ring, number)
        spread(number)
    x_copy(3, z).wait_recv()
    ring_first(far_ring)
    ring_second(z_ring)
    for number in (2, 6):
        spread(number)
    for number in (3, 5, 4):
        ring_wait(z_ring, number)
        spread(number)
    start(twin_copy(0))
    ring_second(far_ring)
    for copy in weights:
        copy.wait_recv()

    def fetch(chunk):
        if chunk == 3:
            for number in (1, 7, 3, 5, 4):
                ring_wait(far_ring, number)
        else:
            for at in range(nz):
                x_copy(BACK[chunk], at).wait_recv()
        start(twin_copy(chunk))

    def pair_copy(chunk, side):
        return remote(
            sb.at[chunk, pl.ds(2 * side, 2)], (pa, pb)[side].at[chunk],
            b_send.at[chunk, side], b_recv.at[chunk, side], y_peer((1, -1)[side]),
        )

    def far_copy(chunk):
        return remote(sb.at[chunk, 4], pc.at[chunk], b_send.at[chunk, 2], b_recv.at[chunk, 2], y_peer(-far))

    def join_copy(chunk, side):
        return remote(
            sc.at[chunk, side], rc.at[chunk, side],
            b_send.at[chunk, 3 + side], b_recv.at[chunk, 3 + side], y_peer((2, -2)[side]),
        )

    def add_features(chunk):
        ours = xg[k, chunk]
        left = ours[:, 0].reshape(rows, width)
        left_grad = ours[:, 1].reshape(rows, width)
        sums = [
            dot(left, wgv[k], 1, 0),
            dot(left, wuv[k], 1, 0),
            dot(left_grad, wdv[k], 1, 1),
        ]
        twin_copy(chunk).wait_recv()
        other = xg[1 - k, chunk]
        right = other[:, 0].reshape(rows, width)
        right_grad = other[:, 1].reshape(rows, width)
        sums[0] += dot(right, wgs[...], 1, 0)
        sums[1] += dot(right, wus[...], 1, 0)
        sums[2] += dot(right_grad, wds[...], 1, 1)
        for part in range(3):
            pf[chunk, :, :, pl.ds(part * half, half)] = sums[part].reshape(ny, block, half)
        for slot, step in enumerate((1, 3, -1, -3, 4)):
            sb[chunk, slot] = encode(pf[chunk, along_y(step)], SUM_SCALE)
        start(far_copy(chunk))
        start(pair_copy(chunk, 0))
        start(pair_copy(chunk, 1))

    def join(chunk):
        pair_copy(chunk, 0).wait_recv()
        pair_copy(chunk, 1).wait_recv()
        far_copy(chunk).wait_recv()
        distant = decode(pc[chunk], SUM_SCALE)
        share = k.astype(jnp.float32)
        ahead = pf[chunk, along_y(2)] + decode(pa[chunk, 1], SUM_SCALE) + distant * share
        behind = pf[chunk, along_y(-2)] + decode(pb[chunk, 1], SUM_SCALE) + distant * (1.0 - share)
        sc[chunk, 0] = encode(ahead, SUM_SCALE)
        sc[chunk, 1] = encode(behind, SUM_SCALE)
        start(join_copy(chunk, 0))
        start(join_copy(chunk, 1))

    def y_ring(chunk):
        return (hb.at[chunk, k], along_y, y_peer, c_send.at[chunk], c_recv.at[chunk])

    def half_copy(chunk):
        ours = hb.at[chunk, k]
        return remote(ours, ours, cs_send.at[chunk], cs_recv.at[chunk], sibling)

    def gate(chunk):
        join_copy(chunk, 0).wait_recv()
        join_copy(chunk, 1).wait_recv()
        total = pf[chunk, y] + decode(pa[chunk, 0], SUM_SCALE) + decode(pb[chunk, 0], SUM_SCALE)
        total += decode(rc[chunk, 0], SUM_SCALE) + decode(rc[chunk, 1], SUM_SCALE)
        gate_pre = total[:, :half]
        up_pre = total[:, half : 2 * half]
        hidden_delta = total[:, 2 * half :]
        sigma = jax.nn.sigmoid(gate_pre)
        silu_gate = gate_pre * sigma
        slope = sigma * (1.0 + gate_pre * (1.0 - sigma))
        hb[chunk, k, y, 0] = (silu_gate * up_pre).astype(jnp.bfloat16)
        hb[chunk, k, y, 1] = (hidden_delta * up_pre * slope).astype(jnp.bfloat16)
        hb[chunk, k, y, 2] = (hidden_delta * silu_gate).astype(jnp.bfloat16)
        ring_first(y_ring(chunk))

    def dx_copy(chunk):
        return remote(
            ib.at[chunk], jb.at[BACK[chunk]], dx_send.at[chunk], dx_recv.at[BACK[chunk]], x_peer(OFFSETS[chunk])
        )

    def term(chunk, side):
        gate_delta = hb[chunk, side, :, 1].reshape(rows, half)
        up_delta = hb[chunk, side, :, 2].reshape(rows, half)
        return dot(gate_delta, wgv[side], 1, 1) + dot(up_delta, wuv[side], 1, 1)

    def share_half(chunk):
        for number in (1, 7, 3, 5, 4):
            ring_wait(y_ring(chunk), number)
        start(half_copy(chunk))

    def grad(chunk):
        total = term(chunk, k)
        half_copy(chunk).wait_recv()
        total = (total + term(chunk, 1 - k)).reshape(nz, block, width)
        if chunk == 0:
            own[...] = total
        else:
            ib[chunk] = encode(total, GRAD_SCALE)
            start(dx_copy(chunk))

    actions = {
        "fetch": fetch, "sum": add_features, "join": join, "gate": gate,
        "pass": lambda chunk: ring_second(y_ring(chunk)), "half": share_half, "grad": grad,
    }
    for name, chunk in STEPS:
        actions[name](chunk)

    for chunk in range(1, nx):
        dx_copy(BACK[chunk]).wait_recv()
    total = own[...]
    for chunk in range(1, nx):
        total += decode(jb[chunk], GRAD_SCALE)
    zf[...] = total
    zs[...] = encode(total, GRAD_SCALE)

    def dz_copy(step):
        return remote(zs.at[along_z(step)], zr.at[step - 1], dz_send.at[step - 1], dz_recv.at[step - 1], z_peer(step))

    for step in (4, 3, 5, 2, 6, 1, 7):
        start(dz_copy(step))

    tokens = nx * rows
    left = xg[k, :, :, 0].reshape(tokens, width)
    for side in range(2):
        cols = pl.ds(side * half, half)
        ggv[:, cols] = dot(left, hb[:, side, :, 1].reshape(tokens, half), 0, 0).astype(jnp.bfloat16)
        ugv[:, cols] = dot(left, hb[:, side, :, 2].reshape(tokens, half), 0, 0).astype(jnp.bfloat16)
    stores = [
        pltpu.make_async_copy(ggv, gg_out, load_sem.at[0]),
        pltpu.make_async_copy(ugv, ug_out, load_sem.at[1]),
        pltpu.make_async_copy(dgv, dg_out, load_sem.at[2]),
        pltpu.make_async_copy(igv, ig_out, load_sem.at[3]),
    ]
    stores[0].start()
    stores[1].start()
    right = xg[k, :, :, 1].reshape(tokens, width)
    for side in range(2):
        cols = pl.ds(side * half, half)
        dgv[cols] = dot(hb[:, side, :, 0].reshape(tokens, half), right, 0, 0).astype(jnp.bfloat16)
    stores[2].start()

    for step in range(1, nz):
        dz_copy(step).wait_recv()
    total = zf[z]
    for step in range(1, nz):
        total += decode(zr[step - 1], GRAD_SCALE)
    igv[...] = total.astype(jnp.bfloat16)
    stores[3].start()

    for copy in sent:
        copy.wait_send()
    for store in stores:
        store.wait()


def hand_over(*refs):
    count = len(refs) // 3
    given, out, held, sems = refs[:count], refs[count : 2 * count], refs[2 * count : 3 * count], refs[-1]
    loads = [pltpu.make_async_copy(given[i], held[i], sems.at[0, i]) for i in range(count)]
    stores = [pltpu.make_async_copy(held[i], out[i], sems.at[1, i]) for i in range(count)]
    for load in loads:
        load.start()
    for load, store in zip(loads, stores):
        load.wait()
        store.start()
    for store in stores:
        store.wait()


def shards(ny, nz, tokens, grad_output, gate_weight, up_weight, down_weight):
    block, width = tokens.shape
    hidden = gate_weight.shape[1] // 2
    half = hidden // 2
    nx = 4
    bf16, f32 = jnp.bfloat16, jnp.float32
    vmem, dma = pltpu.VMEM, pltpu.SemaphoreType.DMA
    results = (
        jax.ShapeDtypeStruct((block, width), bf16),
        jax.ShapeDtypeStruct((width, hidden), bf16),
        jax.ShapeDtypeStruct((width, hidden), bf16),
        jax.ShapeDtypeStruct((hidden, width), bf16),
    )
    made = pl.pallas_call(
        functools.partial(kernel, ny, nz),
        out_shape=results,
        in_specs=[pl.BlockSpec(memory_space=pl.ANY)] * 5,
        out_specs=[pl.BlockSpec(memory_space=pl.ANY)] * 4,
        scratch_shapes=[
            vmem((2, nx, nz, 2, block, width), bf16),
            vmem((2, width, half), bf16),
            vmem((2, width, half), bf16),
            vmem((2, half, width), bf16),
            vmem((width, half), bf16),
            vmem((width, half), bf16),
            vmem((half, width), bf16),
            vmem((nx, ny, block, 3 * half), f32),
            vmem((nx, 5, block, 3 * half), bf16),
            vmem((nx, 2, block, 3 * half), bf16),
            vmem((nx, 2, block, 3 * half), bf16),
            vmem((nx, block, 3 * half), bf16),
            vmem((nx, 2, block, 3 * half), bf16),
            vmem((nx, 2, block, 3 * half), bf16),
            vmem((nx, 2, ny, 3, block, half), bf16),
            vmem((nz, block, width), f32),
            vmem((nx, nz, block, width), bf16),
            vmem((nx, nz, block, width), bf16),
            vmem((nz, block, width), f32),
            vmem((nz, block, width), bf16),
            vmem((nz - 1, block, width), bf16),
            vmem((width, hidden), bf16),
            vmem((width, hidden), bf16),
            vmem((hidden, width), bf16),
            vmem((block, width), bf16),
            dma((8,)),
            dma((2, nz)), dma((2, nz)),
            dma((nx, nz)), dma((nx, nz)),
            dma((nx,)), dma((nx,)),
            dma((3,)), dma((3,)),
            dma((nx, 5)), dma((nx, 5)),
            dma((nx, ny)), dma((nx, ny)),
            dma((nx,)), dma((nx,)),
            dma((nx,)), dma((nx,)),
            dma((nz - 1,)), dma((nz - 1,)),
        ],
        compiler_params=pltpu.CompilerParams(
            collective_id=0, has_side_effects=True, vmem_limit_bytes=60 * 2**20
        ),
        name="ffn_backward",
    )(tokens, grad_output, gate_weight, up_weight, down_weight)
    return pl.pallas_call(
        hand_over,
        out_shape=results,
        in_specs=[pl.BlockSpec(memory_space=pl.ANY)] * 4,
        out_specs=[pl.BlockSpec(memory_space=pl.ANY)] * 4,
        scratch_shapes=[vmem(result.shape, bf16) for result in results] + [dma((2, 4))],
        compiler_params=pltpu.CompilerParams(vmem_limit_bytes=60 * 2**20),
        name="hand_over",
    )(*made)


def solution(mesh):
    placed = (
        P(("col", "depth"), "row"),
        P(("col", "depth"), "row"),
        P("row", "col"),
        P("row", "col"),
        P("col", "row"),
    )
    ny, nz = mesh.shape["row"] // 2, mesh.shape["col"] // 2
    return jax.shard_map(
        functools.partial(shards, ny, nz),
        mesh=mesh,
        in_specs=placed,
        out_specs=(
            P(("col", "depth"), "row"),
            P("row", ("col", "depth")),
            P("row", ("col", "depth")),
            P(("col", "depth"), "row"),
        ),
        check_vma=False,
    )
```

time: 87.6 us -> 71 us (0.81)
  Pallas kernels: 81.4 us -> 69.7 us
  local copies, waits for them, and re-layouts: 5.28 us -> 0 us
    pallas_call x1 -> x2, Pallas kernels: 81.4 us -> 69.7 us  [the longest x1 67.5 us: shards(): pl.pallas_call(functools.partial(kernel, ny, nz), out_shape=results, in_s...]
    unnamed x8 -> x0, local copies, waits for them, and re-layouts: 5.28 us -> none
where the time goes in v2:
time: 71 us; the launch traced here: 70.4 us
  Pallas kernels  69.7 us (98%)
    pallas_call x1, Pallas kernels, shards(): pl.pallas_call(functools.partial(kernel, ny, nz), out_shape=results, in_s...  67.5 us
    pallas_call x1, Pallas kernels, shards(): pl.pallas_call(hand_over, out_shape=results, in_specs=[pl.BlockSpec(memor...  2.27 us

profile of v2, /device:TPU:1, one launch (start us, length us, event | category | flops | bytes accessed | tf_op | source)
XLA Modules:
  0.0 70.4 jit_solution(3406202838091482867)
XLA Ops:
  0.6 67.5 %ffn_backward.1 = (bf16[16,512]{1,0:T(8,128)(2,1)}, bf16[512,512]{1,0:T(8,128)(2,1)}, bf16[512,512]{1,0:T(8,128)(2,1)}, bf16[512,512]{1,0:T(8,128)(2,1)}) custom-call(bf16[16,512]{1,0:T(8,128)(2,1)} %tok.1, bf16[16,512]{1,0:T(8,128)(2,1)} %grd.1, bf16[512,1024]{1,0:T(8,128)(2,1)} %wg.1, bf16[512,1024]{1,0:T(8,128)(2,1)} %wu.1, bf16[1024,512]{1,0:T(8,128)(2,1)} %wd.1), custom_call_target="tpu_custom_call" | custom-call | tf_op jit(solution)/shard_map/ffn_backward/pallas_call | solution.py:368
  68.1 2.3 %hand_over.1 = (bf16[16,512]{1,0:T(8,128)(2,1)}, bf16[512,512]{1,0:T(8,128)(2,1)}, bf16[512,512]{1,0:T(8,128)(2,1)}, bf16[512,512]{1,0:T(8,128)(2,1)}) custom-call(bf16[16,512]{1,0:T(8,128)(2,1)} %get-tuple-element.8.refs_0_, bf16[512,512]{1,0:T(8,128)(2,1)} %get-tuple-element.9.refs_1_, bf16[512,512]{1,0:T(8,128)(2,1)} %get-tuple-element.10.refs_2_, ...), custom_call_target="tpu_custom_call" | custom-call | tf_op jit(solution)/shard_map/hand_over/pallas_call | solution.py:415

commit v3 on v2

v3 whole, which is shorter than its diff:
```python
import functools

import jax
import jax.numpy as jnp
from jax import lax
from jax.experimental import pallas as pl
from jax.experimental.pallas import tpu as pltpu
from jax.sharding import PartitionSpec as P

MESH = pl.DeviceIdType.MESH
OFFSETS = (0, 1, 3, 2)
BACK = (0, 2, 1, 3)
SLOTS = (0, 1, -1, 2, -2, 3, -3, 4)
SUM_SCALE = 2.0**48
GRAD_SCALE = 2.0**30


def encode(value, scale):
    scaled = value * scale
    return (scaled * jnp.abs(scaled)).astype(jnp.bfloat16)


def decode(code, scale):
    wide = code.astype(jnp.float32)
    root = jnp.sqrt(jnp.abs(wide)) * (1.0 / scale)
    return jnp.where(wide < 0.0, -root, root)


def dot(left, right, left_dim, right_dim):
    return lax.dot_general(
        left, right, (((left_dim,), (right_dim,)), ((), ())), preferred_element_type=jnp.float32
    )


STEPS = (
    "near0", "fetch0", "sum0", "fetch2", "fetch4", "far0", "rest0", "sum2", "sum4", "fetch6", "fetch1", "join0",
    "sum6", "sum1", "join2", "join4", "fetch3", "fetch5", "fetch7", "gate0", "join6", "sum3", "sum5", "sum7",
    "join1", "gate2", "gate4", "pass0", "join3", "join5", "join7", "gate6", "pass2", "pass4", "gate3", "half0",
    "pass6", "gate5", "gate7", "gate1", "grad0", "half2", "half4", "grad2", "pass3", "grad4", "half6", "pass5",
    "pass7", "pass1", "grad6", "half3", "half5", "grad3", "half7", "grad5", "half1", "grad7", "grad1", "merge1",
)


def kernel(
    ny, nz,
    tok, grd, wg, wu, wd,
    ig_out, gg_out, ug_out, dg_out,
    xg, wgv, wuv, wdv, wgs, wus, wds, xo, pf, sb, pa, pb, pc, sc, rc, hb, ho, own, ib, jb, mb, tail, ggv, ugv, dgv, igv,
    load_sem, az_send, az_recv, ax_send, ax_recv, as_send, as_recv, ws_send, ws_recv,
    b_send, b_recv, c_send, c_recv, cs_send, cs_recv, dx_send, dx_recv, mx_send, mx_recv,
):
    nx = 4
    block, width = tok.shape
    half = wgv.shape[2]
    blocks = nz // 2
    rows = blocks * block
    share = rows // ny
    cut = half // 2
    r, q, d = lax.axis_index("row"), lax.axis_index("col"), lax.axis_index("depth")
    y, k = r // 2, lax.rem(r, 2)
    z, x = q // 2, d * 2 + lax.rem(q, 2)

    def place(py, pz, px, pk):
        return (py * 2 + pk, pz * 2 + lax.rem(px, 2), px // 2)

    def along_y(step):
        return lax.rem(y + step + ny, ny)

    def along_z(step):
        return lax.rem(z + step + nz, nz)

    def y_peer(step):
        return place(along_y(step), z, x, k)

    def plane_peer(step, across):
        return place(y, along_z(step), lax.rem(x + across, nx), k)

    def z_peer(step):
        return plane_peer(step, 0)

    def x_peer(across):
        return plane_peer(0, across)

    sibling = place(y, z, x, 1 - k)
    far = 2 - 4 * k
    sent = []

    def remote(src, dst, send, recv, device):
        return pltpu.make_async_remote_copy(
            src_ref=src, dst_ref=dst, send_sem=send, recv_sem=recv, device_id=device, device_id_type=MESH
        )

    def start(copy):
        copy.start()
        sent.append(copy)

    loads = [
        pltpu.make_async_copy(tok, xg.at[k, 0, 0, 0], load_sem.at[0]),
        pltpu.make_async_copy(grd, xg.at[k, 0, 0, 1], load_sem.at[1]),
    ]
    for side in range(2):
        first = pl.multiple_of(d * (2 * half) + side * half, half)
        loads += [
            pltpu.make_async_copy(wg.at[:, pl.ds(first, half)], wgv.at[side], load_sem.at[2 + side]),
            pltpu.make_async_copy(wu.at[:, pl.ds(first, half)], wuv.at[side], load_sem.at[4 + side]),
            pltpu.make_async_copy(wd.at[pl.ds(first, half)], wdv.at[side], load_sem.at[6 + side]),
        ]
    for load in loads:
        load.start()

    barrier = pltpu.get_barrier_semaphore()
    friends = [sibling]
    friends += [z_peer(step) for step in (1, -1, 2, -2)]
    friends += [x_peer(across) for across in range(1, nx)]
    friends += [y_peer(step) for step in (1, -1, 2, -2)]
    for device in friends:
        pl.semaphore_signal(barrier, inc=1, device_id=device, device_id_type=MESH)
    loads[0].wait()
    loads[1].wait()
    pl.semaphore_wait(barrier, len(friends))

    def ring_copy(ring, origin, number, target):
        buffer, mine, theirs, peer, send, recv = ring
        return remote(
            buffer.at[mine(origin)], buffer.at[theirs(origin, number)], send.at[number], recv.at[number], peer(target)
        )

    def ring_first(ring):
        for target in (2, -2, 1, -1):
            start(ring_copy(ring, 0, target % 8, target))

    def ring_second(ring):
        ring_wait(ring, 2)
        ring_wait(ring, 6)
        start(ring_copy(ring, None, 4, far))
        start(ring_copy(ring, -2, 3, 1))
        start(ring_copy(ring, 2, 5, -1))

    def ring_wait(ring, number):
        buffer, mine, theirs, peer, send, recv = ring
        place_of = buffer.at[theirs(-number, number)]
        remote(place_of, place_of, send.at[number], recv.at[number], peer(1)).wait_recv()

    def slot(origin):
        return SLOTS.index((origin + 3) % 8 - 3)

    def z_mine(origin):
        return slot(2) * k + slot(-2) * (1 - k) if origin is None else slot(origin)

    def z_ring(column, which):
        return (
            xg.at[k, column], z_mine, lambda origin, number: slot(-number), z_peer, az_send.at[which], az_recv.at[which]
        )

    own_ring, far_ring = z_ring(0, 0), z_ring(3, 1)

    def x_copy(column, at):
        return remote(
            xg.at[k, 0, at], xg.at[k, BACK[column], at],
            ax_send.at[column, at], ax_recv.at[BACK[column], at], x_peer(OFFSETS[column]),
        )

    def twin_copy(chunk):
        ours = xg.at[k, chunk // 2, pl.ds(chunk % 2 * blocks, blocks)]
        return remote(ours, ours, as_send.at[chunk], as_recv.at[chunk], sibling)

    def spread(origin):
        for column in (1, 2):
            start(x_copy(column, slot(origin)))

    start(x_copy(3, 0))
    ring_first(own_ring)
    spread(0)
    for load in loads[2:]:
        load.wait()
    weights = [
        remote(wgv.at[1 - k], wgs, ws_send.at[0], ws_recv.at[0], sibling),
        remote(wuv.at[1 - k], wus, ws_send.at[1], ws_recv.at[1], sibling),
        remote(wdv.at[1 - k], wds, ws_send.at[2], ws_recv.at[2], sibling),
    ]
    for copy in weights:
        start(copy)

    def near(_):
        ring_wait(own_ring, 1)
        ring_wait(own_ring, 7)
        spread(-1)
        spread(1)
        x_copy(3, 0).wait_recv()
        ring_first(far_ring)
        ring_second(own_ring)
        spread(2)
        spread(-2)

    def rest(_):
        for number in (3, 5, 4):
            ring_wait(own_ring, number)
            spread(-number)

    def fetch(chunk):
        column, part = chunk // 2, chunk % 2
        for origin in SLOTS[part * blocks : (part + 1) * blocks]:
            if column in (1, 2):
                x_copy(BACK[column], slot(origin)).wait_recv()
            elif column == 3 and origin in (1, -1, 3, -3, 4):
                ring_wait(far_ring, -origin % 8)
        start(twin_copy(chunk))

    def pair_copy(chunk, side):
        return remote(
            sb.at[chunk, pl.ds(2 * side, 2)], (pa, pb)[side].at[chunk],
            b_send.at[chunk, side], b_recv.at[chunk, side], y_peer((1, -1)[side]),
        )

    def far_copy(chunk):
        return remote(sb.at[chunk, 4], pc.at[chunk], b_send.at[chunk, 2], b_recv.at[chunk, 2], y_peer(-far))

    def join_copy(chunk, side):
        return remote(
            sc.at[chunk, side], rc.at[chunk, side],
            b_send.at[chunk, 3 + side], b_recv.at[chunk, 3 + side], y_peer((2, -2)[side]),
        )

    def add_features(chunk):
        column, slots = chunk // 2, pl.ds(chunk % 2 * blocks, blocks)
        ours = xg[k, column, slots]
        left = ours[:, 0].reshape(rows, width)
        left_grad = ours[:, 1].reshape(rows, width)
        xo[0, chunk] = left
        xo[1, chunk] = left_grad
        sums = [
            dot(left, wgv[k], 1, 0),
            dot(left, wuv[k], 1, 0),
            dot(left_grad, wdv[k], 1, 1),
        ]
        if chunk == 0:
            for copy in weights:
                copy.wait_recv()
        twin_copy(chunk).wait_recv()
        other = xg[1 - k, column, slots]
        right = other[:, 0].reshape(rows, width)
        right_grad = other[:, 1].reshape(rows, width)
        sums[0] += dot(right, wgs[...], 1, 0)
        sums[1] += dot(right, wus[...], 1, 0)
        sums[2] += dot(right_grad, wds[...], 1, 1)
        for part in range(3):
            cols = pl.ds(part * cut, cut)
            for side in range(2):
                pf[chunk, :, pl.ds(side * share, share), cols] = sums[part][:, side * cut : (side + 1) * cut].reshape(
                    ny, share, cut
                )
        for index, step in enumerate((1, 3, -1, -3, 4)):
            sb[chunk, index] = encode(pf[chunk, along_y(step)], SUM_SCALE)
        start(far_copy(chunk))
        start(pair_copy(chunk, 0))
        start(pair_copy(chunk, 1))

    def join(chunk):
        pair_copy(chunk, 0).wait_recv()
        pair_copy(chunk, 1).wait_recv()
        far_copy(chunk).wait_recv()
        distant = decode(pc[chunk], SUM_SCALE)
        second = k.astype(jnp.float32)
        ahead = pf[chunk, along_y(2)] + decode(pa[chunk, 1], SUM_SCALE) + distant * second
        behind = pf[chunk, along_y(-2)] + decode(pb[chunk, 1], SUM_SCALE) + distant * (1.0 - second)
        sc[chunk, 0] = encode(ahead, SUM_SCALE)
        sc[chunk, 1] = encode(behind, SUM_SCALE)
        start(join_copy(chunk, 0))
        start(join_copy(chunk, 1))

    def y_ring(chunk):
        def mine(origin):
            return along_y(-far if origin is None else origin)

        return (hb.at[chunk, k], mine, lambda origin, _: mine(origin), y_peer, c_send.at[chunk], c_recv.at[chunk])

    def half_copy(chunk):
        ours = hb.at[chunk, k]
        return remote(ours, ours, cs_send.at[chunk], cs_recv.at[chunk], sibling)

    def gate(chunk):
        join_copy(chunk, 0).wait_recv()
        join_copy(chunk, 1).wait_recv()
        total = pf[chunk, y] + decode(pa[chunk, 0], SUM_SCALE) + decode(pb[chunk, 0], SUM_SCALE)
        total += decode(rc[chunk, 0], SUM_SCALE) + decode(rc[chunk, 1], SUM_SCALE)
        gate_pre = total[:, :cut]
        up_pre = total[:, cut : 2 * cut]
        hidden_delta = total[:, 2 * cut :]
        sigma = jax.nn.sigmoid(gate_pre)
        silu_gate = gate_pre * sigma
        slope = sigma * (1.0 + gate_pre * (1.0 - sigma))
        hb[chunk, k, y, 0] = (silu_gate * up_pre).astype(jnp.bfloat16)
        hb[chunk, k, y, 1] = (hidden_delta * up_pre * slope).astype(jnp.bfloat16)
        hb[chunk, k, y, 2] = (hidden_delta * silu_gate).astype(jnp.bfloat16)
        ring_first(y_ring(chunk))

    def block_copy(column, chunk, index):
        step = SLOTS[index] % nz
        return remote(
            ib.at[chunk, index % blocks], jb.at[BACK[column], step],
            dx_send.at[column, step], dx_recv.at[BACK[column], step], plane_peer(step, OFFSETS[column]),
        )

    def term(chunk, side):
        for array in range(3):
            pieces = hb[chunk, side, :, array].astype(jnp.float32)
            first = pieces[:, :share].reshape(rows, cut)
            second = pieces[:, share:].reshape(rows, cut)
            ho[array, side, chunk] = jnp.concatenate([first, second], axis=1).astype(jnp.bfloat16)
        return dot(ho[1, side, chunk], wgv[side], 1, 1) + dot(ho[2, side, chunk], wuv[side], 1, 1)

    def share_half(chunk):
        for number in (1, 7, 3, 5, 4):
            ring_wait(y_ring(chunk), number)
        start(half_copy(chunk))

    def grad(chunk):
        total = term(chunk, k)
        half_copy(chunk).wait_recv()
        total = (total + term(chunk, 1 - k)).reshape(blocks, block, width)
        if chunk == 1:
            tail[...] = total
            return
        ib[chunk] = encode(total, GRAD_SCALE)
        if chunk == 0:
            own[...] = total[0]
        if chunk in (3, 5):
            start(column_copy(chunk // 2))
        else:
            send_blocks(chunk)

    def send_blocks(chunk):
        column, part = chunk // 2, chunk % 2
        for index in reversed(range(part * blocks, (part + 1) * blocks)):
            if column or index:
                start(block_copy(column, chunk, index))

    def column_copy(column):
        return remote(
            ib.at[2 * column + 1], mb.at[BACK[column] - 1],
            mx_send.at[column - 1], mx_recv.at[BACK[column] - 1], x_peer(OFFSETS[column]),
        )

    def merge(chunk):
        total = tail[...]
        for column in (1, 2):
            column_copy(BACK[column]).wait_recv()
            total += decode(mb[column - 1], GRAD_SCALE)
        ib[chunk] = encode(total, GRAD_SCALE)
        send_blocks(chunk)

    actions = {
        "near": near, "far": lambda _: ring_second(far_ring), "rest": rest,
        "fetch": fetch, "sum": add_features, "join": join, "gate": gate,
        "pass": lambda chunk: ring_second(y_ring(chunk)), "half": share_half, "grad": grad,
        "merge": merge,
    }
    for step in STEPS:
        actions[step[:-1]](int(step[-1]))

    tokens = 2 * nx * rows
    left = xo[0].reshape(tokens, width)
    for side in range(2):
        cols = pl.ds(side * half, half)
        ggv[:, cols] = dot(left, ho[1, side].reshape(tokens, half), 0, 0).astype(jnp.bfloat16)
        ugv[:, cols] = dot(left, ho[2, side].reshape(tokens, half), 0, 0).astype(jnp.bfloat16)
    stores = [
        pltpu.make_async_copy(ggv, gg_out, load_sem.at[0]),
        pltpu.make_async_copy(ugv, ug_out, load_sem.at[1]),
        pltpu.make_async_copy(dgv, dg_out, load_sem.at[2]),
        pltpu.make_async_copy(igv, ig_out, load_sem.at[3]),
    ]
    stores[0].start()
    stores[1].start()
    right = xo[1].reshape(tokens, width)
    for side in range(2):
        cols = pl.ds(side * half, half)
        dgv[cols] = dot(ho[0, side].reshape(tokens, half), right, 0, 0).astype(jnp.bfloat16)
    stores[2].start()

    for copy in sent:
        copy.wait_send()
    total = own[...]
    for column in (1, 2, 3, 0):
        for index in range(nz if column in (0, 3) else blocks):
            if column or index:
                block_copy(BACK[column], 0, index).wait_recv()
                total += decode(jb[column, SLOTS[index] % nz], GRAD_SCALE)
    igv[...] = total.astype(jnp.bfloat16)
    stores[3].start()
    for store in stores:
        store.wait()


def hand_over(*refs):
    count = len(refs) // 3
    given, out, held, sems = refs[:count], refs[count : 2 * count], refs[2 * count : 3 * count], refs[-1]
    loads = [pltpu.make_async_copy(given[i], held[i], sems.at[0, i]) for i in range(count)]
    stores = [pltpu.make_async_copy(held[i], out[i], sems.at[1, i]) for i in range(count)]
    for load in loads:
        load.start()
    for load, store in zip(loads, stores):
        load.wait()
        store.start()
    for store in stores:
        store.wait()


def shards(ny, nz, tokens, grad_output, gate_weight, up_weight, down_weight):
    block, width = tokens.shape
    hidden = gate_weight.shape[1] // 2
    half = hidden // 2
    nx = 4
    chunks, rows, cut = 2 * nx, nz // 2 * block, half // 2
    bf16, f32 = jnp.bfloat16, jnp.float32
    vmem, dma = pltpu.VMEM, pltpu.SemaphoreType.DMA
    results = (
        jax.ShapeDtypeStruct((block, width), bf16),
        jax.ShapeDtypeStruct((width, hidden), bf16),
        jax.ShapeDtypeStruct((width, hidden), bf16),
        jax.ShapeDtypeStruct((hidden, width), bf16),
    )
    made = pl.pallas_call(
        functools.partial(kernel, ny, nz),
        out_shape=results,
        in_specs=[pl.BlockSpec(memory_space=pl.ANY)] * 5,
        out_specs=[pl.BlockSpec(memory_space=pl.ANY)] * 4,
        scratch_shapes=[
            vmem((2, nx, nz, 2, block, width), bf16),
            vmem((2, width, half), bf16),
            vmem((2, width, half), bf16),
            vmem((2, half, width), bf16),
            vmem((width, half), bf16),
            vmem((width, half), bf16),
            vmem((half, width), bf16),
            vmem((2, chunks, rows, width), bf16),
            vmem((chunks, ny, block, 3 * cut), f32),
            vmem((chunks, 5, block, 3 * cut), bf16),
            vmem((chunks, 2, block, 3 * cut), bf16),
            vmem((chunks, 2, block, 3 * cut), bf16),
            vmem((chunks, block, 3 * cut), bf16),
            vmem((chunks, 2, block, 3 * cut), bf16),
            vmem((chunks, 2, block, 3 * cut), bf16),
            vmem((chunks, 2, ny, 3, block, cut), bf16),
            vmem((3, 2, chunks, rows, half), bf16),
            vmem((block, width), f32),
            vmem((chunks, nz // 2, block, width), bf16),
            vmem((nx, nz, block, width), bf16),
            vmem((2, nz // 2, block, width), bf16),
            vmem((nz // 2, block, width), f32),
            vmem((width, hidden), bf16),
            vmem((width, hidden), bf16),
            vmem((hidden, width), bf16),
            vmem((block, width), bf16),
            dma((8,)),
            dma((2, nz)), dma((2, nz)),
            dma((nx, nz)), dma((nx, nz)),
            dma((chunks,)), dma((chunks,)),
            dma((3,)), dma((3,)),
            dma((chunks, 5)), dma((chunks, 5)),
            dma((chunks, ny)), dma((chunks, ny)),
            dma((chunks,)), dma((chunks,)),
            dma((nx, nz)), dma((nx, nz)),
            dma((2,)), dma((2,)),
        ],
        compiler_params=pltpu.CompilerParams(
            collective_id=0, has_side_effects=True, vmem_limit_bytes=60 * 2**20
        ),
        name="ffn_backward",
    )(tokens, grad_output, gate_weight, up_weight, down_weight)
    return pl.pallas_call(
        hand_over,
        out_shape=results,
        in_specs=[pl.BlockSpec(memory_space=pl.ANY)] * 4,
        out_specs=[pl.BlockSpec(memory_space=pl.ANY)] * 4,
        scratch_shapes=[vmem(result.shape, bf16) for result in results] + [dma((2, 4))],
        compiler_params=pltpu.CompilerParams(vmem_limit_bytes=60 * 2**20),
        name="hand_over",
    )(*made)


def solution(mesh):
    placed = (
        P(("col", "depth"), "row"),
        P(("col", "depth"), "row"),
        P("row", "col"),
        P("row", "col"),
        P("col", "row"),
    )
    ny, nz = mesh.shape["row"] // 2, mesh.shape["col"] // 2
    return jax.shard_map(
        functools.partial(shards, ny, nz),
        mesh=mesh,
        in_specs=placed,
        out_specs=(
            P(("col", "depth"), "row"),
            P("row", ("col", "depth")),
            P("row", ("col", "depth")),
            P(("col", "depth"), "row"),
        ),
        check_vma=False,
    )
```

time: 71 us -> 66 us (0.930)
  Pallas kernels: 69.7 us -> 65.1 us
    pallas_call x1, Pallas kernels: 67.5 us -> 62.8 us  [shards(): pl.pallas_call(functools.partial(kernel, ny, nz), out_shape=results, in_s...]
where the time goes in v3:
time: 66 us; the launch traced here: 65.7 us
  Pallas kernels  65.1 us (99%)
    pallas_call x1, Pallas kernels, shards(): pl.pallas_call(functools.partial(kernel, ny, nz), out_shape=results, in_s...  62.8 us
    pallas_call x1, Pallas kernels, shards(): pl.pallas_call(hand_over, out_shape=results, in_specs=[pl.BlockSpec(memor...  2.27 us

profile of v3, /device:TPU:1, one launch (start us, length us, event | category | flops | bytes accessed | tf_op | source)
XLA Modules:
  0.0 65.7 jit_solution(16980619337158738678)
XLA Ops:
  0.6 62.8 %ffn_backward.1 = (bf16[16,512]{1,0:T(8,128)(2,1)}, bf16[512,512]{1,0:T(8,128)(2,1)}, bf16[512,512]{1,0:T(8,128)(2,1)}, bf16[512,512]{1,0:T(8,128)(2,1)}) custom-call(bf16[16,512]{1,0:T(8,128)(2,1)} %tok.1, bf16[16,512]{1,0:T(8,128)(2,1)} %grd.1, bf16[512,1024]{1,0:T(8,128)(2,1)} %wg.1, bf16[512,1024]{1,0:T(8,128)(2,1)} %wu.1, bf16[1024,512]{1,0:T(8,128)(2,1)} %wd.1), custom_call_target="tpu_custom_call" | custom-call | tf_op jit(solution)/shard_map/ffn_backward/pallas_call | solution.py:423
  63.4 2.3 %hand_over.1 = (bf16[16,512]{1,0:T(8,128)(2,1)}, bf16[512,512]{1,0:T(8,128)(2,1)}, bf16[512,512]{1,0:T(8,128)(2,1)}, bf16[512,512]{1,0:T(8,128)(2,1)}) custom-call(bf16[16,512]{1,0:T(8,128)(2,1)} %get-tuple-element.8.refs_0_, bf16[512,512]{1,0:T(8,128)(2,1)} %get-tuple-element.9.refs_1_, bf16[512,512]{1,0:T(8,128)(2,1)} %get-tuple-element.10.refs_2_, ...), custom_call_target="tpu_custom_call" | custom-call | tf_op jit(solution)/shard_map/hand_over/pallas_call | solution.py:471

commit v4 on v3

--- a/solution.py
+++ b/solution.py
@@ -45,7 +45,7 @@
     ny, nz,
     tok, grd, wg, wu, wd,
     ig_out, gg_out, ug_out, dg_out,
-    xg, wgv, wuv, wdv, wgs, wus, wds, xo, pf, sb, pa, pb, pc, sc, rc, hb, ho, own, ib, jb, mb, tail, ggv, ugv, dgv, igv,
+    xg, wgv, wuv, wdv, wgs, wus, wds, wgt, wut, wdt, xo, pf, sb, pa, pb, pc, sc, rc, hb, ho, own, ib, jb, mb, tail, ggv, ugv, dgv, igv,
     load_sem, az_send, az_recv, ax_send, ax_recv, as_send, as_recv, ws_send, ws_recv,
     b_send, b_recv, c_send, c_recv, cs_send, cs_recv, dx_send, dx_recv, mx_send, mx_recv,
 ):
@@ -176,10 +176,16 @@
     weights = [
         remote(wgv.at[1 - k], wgs, ws_send.at[0], ws_recv.at[0], sibling),
         remote(wuv.at[1 - k], wus, ws_send.at[1], ws_recv.at[1], sibling),
-        remote(wdv.at[1 - k], wds, ws_send.at[2], ws_recv.at[2], sibling),
+        remote(wdt.at[1 - k], wds, ws_send.at[2], ws_recv.at[2], sibling),
     ]
-    for copy in weights:
-        start(copy)
+    start(weights[0])
+    start(weights[1])
+    wdt[1 - k] = wdv[1 - k].T
+    start(weights[2])
+    wdt[k] = wdv[k].T
+    for side in range(2):
+        wgt[side] = wgv[side].T
+        wut[side] = wuv[side].T
 
     def near(_):
         ring_wait(own_ring, 1)
@@ -231,7 +237,7 @@
         sums = [
             dot(left, wgv[k], 1, 0),
             dot(left, wuv[k], 1, 0),
-            dot(left_grad, wdv[k], 1, 1),
+            dot(left_grad, wdt[k], 1, 0),
         ]
         if chunk == 0:
             for copy in weights:
@@ -242,7 +248,7 @@
         right_grad = other[:, 1].reshape(rows, width)
         sums[0] += dot(right, wgs[...], 1, 0)
         sums[1] += dot(right, wus[...], 1, 0)
-        sums[2] += dot(right_grad, wds[...], 1, 1)
+        sums[2] += dot(right_grad, wds[...], 1, 0)
         for part in range(3):
             cols = pl.ds(part * cut, cut)
             for side in range(2):
@@ -307,7 +313,7 @@
             first = pieces[:, :share].reshape(rows, cut)
             second = pieces[:, share:].reshape(rows, cut)
             ho[array, side, chunk] = jnp.concatenate([first, second], axis=1).astype(jnp.bfloat16)
-        return dot(ho[1, side, chunk], wgv[side], 1, 1) + dot(ho[2, side, chunk], wuv[side], 1, 1)
+        return dot(ho[1, side, chunk], wgt[side], 1, 0) + dot(ho[2, side, chunk], wut[side], 1, 0)
 
     def share_half(chunk):
         for number in (1, 7, 3, 5, 4):
@@ -432,7 +438,10 @@
             vmem((2, half, width), bf16),
             vmem((width, half), bf16),
             vmem((width, half), bf16),
-            vmem((half, width), bf16),
+            vmem((width, half), bf16),
+            vmem((2, half, width), bf16),
+            vmem((2, half, width), bf16),
+            vmem((2, width, half), bf16),
             vmem((2, chunks, rows, width), bf16),
             vmem((chunks, ny, block, 3 * cut), f32),
             vmem((chunks, 5, block, 3 * cut), bf16),

time: 66 us -> 65 us (0.985)
  Pallas kernels: 65.1 us -> 64.1 us
    pallas_call x1, Pallas kernels: 62.8 us -> 61.8 us  [shards(): pl.pallas_call(functools.partial(kernel, ny, nz), out_shape=results, in_s...]
where the time goes in v4:
time: 65 us; the launch traced here: 64.7 us
  Pallas kernels  64.1 us (99%)
    pallas_call x1, Pallas kernels, shards(): pl.pallas_call(functools.partial(kernel, ny, nz), out_shape=results, in_s...  61.8 us
    pallas_call x1, Pallas kernels, shards(): pl.pallas_call(hand_over, out_shape=results, in_specs=[pl.BlockSpec(memor...  2.27 us

profile of v4, /device:TPU:1, one launch (start us, length us, event | category | flops | bytes accessed | tf_op | source)
XLA Modules:
  0.0 64.7 jit_solution(12081039432568664336)
XLA Ops:
  0.6 61.8 %ffn_backward.1 = (bf16[16,512]{1,0:T(8,128)(2,1)}, bf16[512,512]{1,0:T(8,128)(2,1)}, bf16[512,512]{1,0:T(8,128)(2,1)}, bf16[512,512]{1,0:T(8,128)(2,1)}) custom-call(bf16[16,512]{1,0:T(8,128)(2,1)} %tok.1, bf16[16,512]{1,0:T(8,128)(2,1)} %grd.1, bf16[512,1024]{1,0:T(8,128)(2,1)} %wg.1, bf16[512,1024]{1,0:T(8,128)(2,1)} %wu.1, bf16[1024,512]{1,0:T(8,128)(2,1)} %wd.1), custom_call_target="tpu_custom_call" | custom-call | tf_op jit(solution)/shard_map/ffn_backward/pallas_call | solution.py:429
  62.5 2.3 %hand_over.1 = (bf16[16,512]{1,0:T(8,128)(2,1)}, bf16[512,512]{1,0:T(8,128)(2,1)}, bf16[512,512]{1,0:T(8,128)(2,1)}, bf16[512,512]{1,0:T(8,128)(2,1)}) custom-call(bf16[16,512]{1,0:T(8,128)(2,1)} %get-tuple-element.8.refs_0_, bf16[512,512]{1,0:T(8,128)(2,1)} %get-tuple-element.9.refs_1_, bf16[512,512]{1,0:T(8,128)(2,1)} %get-tuple-element.10.refs_2_, ...), custom_call_target="tpu_custom_call" | custom-call | tf_op jit(solution)/shard_map/hand_over/pallas_call | solution.py:480

commit v5 on v4

--- a/solution.py
+++ b/solution.py
@@ -32,12 +32,13 @@
     )
 
 
+LAST = 1
 STEPS = (
     "near0", "fetch0", "sum0", "fetch2", "fetch4", "far0", "rest0", "sum2", "sum4", "fetch6", "fetch1", "join0",
     "sum6", "sum1", "join2", "join4", "fetch3", "fetch5", "fetch7", "gate0", "join6", "sum3", "sum5", "sum7",
     "join1", "gate2", "gate4", "pass0", "join3", "join5", "join7", "gate6", "pass2", "pass4", "gate3", "half0",
     "pass6", "gate5", "gate7", "gate1", "grad0", "half2", "half4", "grad2", "pass3", "grad4", "half6", "pass5",
-    "pass7", "pass1", "grad6", "half3", "half5", "grad3", "half7", "grad5", "half1", "grad7", "grad1", "merge1",
+    "pass7", "grad6", "half3", "half5", "grad3", "half7", "grad5", "half1", "grad7", "grad1", "merge1",
 )
 
 
@@ -135,6 +136,10 @@
         start(ring_copy(ring, None, 4, far))
         start(ring_copy(ring, -2, 3, 1))
         start(ring_copy(ring, 2, 5, -1))
+
+    def ring_all(ring):
+        for target in (4, 3, -3, 2, -2, 1, -1):
+            start(ring_copy(ring, 0, target % 8, target))
 
     def ring_wait(ring, number):
         buffer, mine, theirs, peer, send, recv = ring
@@ -298,7 +303,10 @@
         hb[chunk, k, y, 0] = (silu_gate * up_pre).astype(jnp.bfloat16)
         hb[chunk, k, y, 1] = (hidden_delta * up_pre * slope).astype(jnp.bfloat16)
         hb[chunk, k, y, 2] = (hidden_delta * silu_gate).astype(jnp.bfloat16)
-        ring_first(y_ring(chunk))
+        if chunk == LAST:
+            ring_all(y_ring(chunk))
+        else:
+            ring_first(y_ring(chunk))
 
     def block_copy(column, chunk, index):
         step = SLOTS[index] % nz
@@ -316,7 +324,7 @@
         return dot(ho[1, side, chunk], wgt[side], 1, 0) + dot(ho[2, side, chunk], wut[side], 1, 0)
 
     def share_half(chunk):
-        for number in (1, 7, 3, 5, 4):
+        for number in (1, 7, 2, 6, 3, 5, 4) if chunk == LAST else (1, 7, 3, 5, 4):
             ring_wait(y_ring(chunk), number)
         start(half_copy(chunk))
 

time: 65 us -> 65.6 us (level)
  no operation moved by 1% of the time
where the time goes in v5:
time: 65.6 us; the launch traced here: 65.3 us
  Pallas kernels  64.7 us (99%)
    pallas_call x1, Pallas kernels, shards(): pl.pallas_call(functools.partial(kernel, ny, nz), out_shape=results, in_s...  62.4 us
    pallas_call x1, Pallas kernels, shards(): pl.pallas_call(hand_over, out_shape=results, in_specs=[pl.BlockSpec(memor...  2.27 us

profile of v5, /device:TPU:1, one launch (start us, length us, event | category | flops | bytes accessed | tf_op | source)
XLA Modules:
  0.0 65.3 jit_solution(5041093766178128804)
XLA Ops:
  0.6 62.4 %ffn_backward.1 = (bf16[16,512]{1,0:T(8,128)(2,1)}, bf16[512,512]{1,0:T(8,128)(2,1)}, bf16[512,512]{1,0:T(8,128)(2,1)}, bf16[512,512]{1,0:T(8,128)(2,1)}) custom-call(bf16[16,512]{1,0:T(8,128)(2,1)} %tok.1, bf16[16,512]{1,0:T(8,128)(2,1)} %grd.1, bf16[512,1024]{1,0:T(8,128)(2,1)} %wg.1, bf16[512,1024]{1,0:T(8,128)(2,1)} %wu.1, bf16[1024,512]{1,0:T(8,128)(2,1)} %wd.1), custom_call_target="tpu_custom_call" | custom-call | tf_op jit(solution)/shard_map/ffn_backward/pallas_call | solution.py:437
  63.0 2.3 %hand_over.1 = (bf16[16,512]{1,0:T(8,128)(2,1)}, bf16[512,512]{1,0:T(8,128)(2,1)}, bf16[512,512]{1,0:T(8,128)(2,1)}, bf16[512,512]{1,0:T(8,128)(2,1)}) custom-call(bf16[16,512]{1,0:T(8,128)(2,1)} %get-tuple-element.8.refs_0_, bf16[512,512]{1,0:T(8,128)(2,1)} %get-tuple-element.9.refs_1_, bf16[512,512]{1,0:T(8,128)(2,1)} %get-tuple-element.10.refs_2_, ...), custom_call_target="tpu_custom_call" | custom-call | tf_op jit(solution)/shard_map/hand_over/pallas_call | solution.py:488
